TPU v7x, 256 devices: a whole 4x4x8 slice. The times are simulated.
256 devices in a mesh: rows: 128 (over x_lo, y, z, core), cols: 2 (over x_hi).
Axes of the slice: x: 4 (x_hi: 2, x_lo: 2; x = x_hi * 2 + x_lo), y: 4, z: 8, core: 2. Of those that a mesh axis runs over, the one named last changes fastest.
Arguments:
- features: bfloat16 [32768, 128], P('rows', 'cols'), may hold values from -6 to 6
- adj_tiles: bfloat16 [12288, 128, 128], P('rows'), may hold values from -0.109375 to 0.109375
- tile_src: int32 [12288], P('rows'), may hold values from 0 to 255, as said below
- tile_dst: int32 [12288], P('rows'), may hold values from 0 to 1, as said below
- tile_count: int32 [128], P('rows'), may hold values from 24 to 96, as said below
- cluster_size: int32 [256], P('rows'), may hold values from 64 to 128, as said below
- weight: bfloat16 [128, 256], P(None, 'cols'), may hold values from -0.5 to 0.5
- bias: float32 [256], P('cols'), may hold values from -3 to 3
- grad_out: bfloat16 [32768, 256], P('rows', 'cols'), may hold values from -6 to 6
Outputs:
- hidden: bfloat16 [32768, 256], P('rows', 'cols')
- grad_weight: float32 [128, 256], P(None, 'cols')
- grad_bias: float32 [256], P('cols')
- grad_features: bfloat16 [32768, 128], P('rows', 'cols')
Inputs may be any that keep to these rules, and one draw needn't show every extreme that they name: In row group r, slots 0 to tile_count[r] - 1 of its 96 slots hold tiles, in non-decreasing order of tile_src; the later slots are unused: their tile_src and tile_dst hold 0, and their adj_tiles hold arbitrary values that must not contribute. A used slot's column cluster belongs to row group r itself or to a row group whose index differs from r in exactly one bit (row group g holds clusters g * 2 to g * 2 + 1). Equal (row, column) pairs may repeat and then add. `tile_dst`: unused slots hold 0. `tile_count`: some row groups use all 96 slots. `cluster_size`: the real nodes of a cluster are its first ones; some cluster is full.
All inputs are finite; a program needn't handle non-finite values.
Results may differ from a plain program's by a relative error of at most 0.006.
Values may be sent and summed in bfloat16 or wider, within the bound.
A program may use at most 64 MiB of HBM per device.

v0:
```python
import math

import jax
import jax.numpy as jnp
from jax import lax
from jax.sharding import PartitionSpec as P

TILE_GROUP = 16


def sweep_slots(first_slot, last_slot, work, totals):
    turn_count = (last_slot - first_slot + TILE_GROUP - 1) // TILE_GROUP

    def one_turn(turn_index, carried):
        slot_ids = first_slot + turn_index * TILE_GROUP + jnp.arange(TILE_GROUP, dtype=jnp.int32)
        return work(carried, slot_ids, slot_ids < last_slot)

    return lax.fori_loop(0, jnp.maximum(turn_count, 0), one_turn, totals)


def slot_bounds(sources, first_slot, last_slot, low_cluster, high_cluster):
    positions = jnp.arange(sources.shape[0], dtype=jnp.int32)
    inside = (positions >= first_slot) & (positions < last_slot)
    below_low = jnp.sum((inside & (sources < low_cluster)).astype(jnp.int32))
    below_high = jnp.sum((inside & (sources < high_cluster)).astype(jnp.int32))
    return (first_slot + below_low, first_slot + below_high)


def gather_products(
    totals, tile_data, sources, targets, slot_ids, is_valid, row_table, base_cluster
):
    clamped = jnp.minimum(slot_ids, tile_data.shape[0] - 1)
    tile_block = tile_data[clamped]
    from_rows = jnp.clip(sources[clamped] - base_cluster, 0, row_table.shape[0] - 1)
    products = jnp.einsum(
        "tij,tjf->tif", tile_block, row_table[from_rows], preferred_element_type=jnp.float32
    )
    placed = jnp.where(is_valid, targets[clamped], totals.shape[0])
    return totals.at[placed].add(products, mode="drop")


def spread_products(totals, tile_data, sources, targets, slot_ids, is_valid, grad_table):
    clamped = jnp.minimum(slot_ids, tile_data.shape[0] - 1)
    tile_block = tile_data[clamped]
    products = jnp.einsum(
        "tji,tjf->tif", tile_block, grad_table[targets[clamped]], preferred_element_type=jnp.float32
    )
    placed = jnp.where(is_valid, sources[clamped], totals.shape[0])
    return totals.at[placed].add(products, mode="drop")


def local(
    features, adj_tiles, tile_src, tile_dst, tile_count, cluster_size, weight, bias, grad_out
):
    clusters_here = cluster_size.shape[0]
    tile_width = adj_tiles.shape[1]
    feat_half = features.shape[1]
    node_rows = clusters_here * tile_width
    node_ids = jnp.arange(tile_width, dtype=jnp.int32)
    live_node = (node_ids[None, :] < cluster_size[:, None]).astype(jnp.float32)[:, :, None]
    live_flat = live_node.reshape(node_rows, 1)
    masked = (
        features.reshape(clusters_here, tile_width, feat_half).astype(jnp.float32) * live_node
    ).astype(jnp.bfloat16)
    my_count = tile_count[0]
    zero_totals = jnp.zeros((clusters_here, tile_width, feat_half), jnp.float32)
    whole_rows = lax.all_gather(masked, "rows", axis=0, tiled=True)
    row_count = whole_rows.shape[0]
    first_slot, last_slot = slot_bounds(tile_src, 0, my_count, 0, 0 + row_count)
    own_totals = sweep_slots(
        first_slot,
        last_slot,
        lambda totals, slot_ids, is_valid: gather_products(
            totals, adj_tiles, tile_src, tile_dst, slot_ids, is_valid, whole_rows, 0
        ),
        zero_totals,
    )
    agg_local = own_totals.reshape(node_rows, feat_half).astype(jnp.bfloat16)
    agg_full = lax.all_gather(agg_local, "cols", axis=1, tiled=True)
    pre_activation = jnp.dot(agg_full, weight, preferred_element_type=jnp.float32) + bias
    sigmoid_pre = jax.nn.sigmoid(pre_activation)
    hidden = (pre_activation * sigmoid_pre * live_flat).astype(jnp.bfloat16)
    grad_pre = (
        grad_out.astype(jnp.float32)
        * sigmoid_pre
        * (1.0 + pre_activation * (1.0 - sigmoid_pre))
        * live_flat
    ).astype(jnp.bfloat16)
    weight_term = lax.dot_general(
        agg_full, grad_pre, (((0,), (0,)), ((), ())), preferred_element_type=jnp.float32
    )
    bias_term = jnp.sum(grad_pre.astype(jnp.float32), axis=0)
    weight_total, bias_total = lax.psum((weight_term, bias_term), "rows")
    grad_scale = 1.0 / math.sqrt(node_rows * lax.axis_size("rows"))
    grad_weight = weight_total * grad_scale
    grad_bias = bias_total * grad_scale
    partial_value = lax.dot_general(
        grad_pre, weight, (((1,), (1,)), ((), ())), preferred_element_type=jnp.float32
    )
    grad_agg = (
        lax.psum_scatter(partial_value, "cols", scatter_dimension=1, tiled=True)
        .astype(jnp.bfloat16)
        .reshape(clusters_here, tile_width, feat_half)
    )
    start_row = jnp.int32(0)
    totals = jnp.zeros((clusters_here * lax.axis_size("rows"), tile_width, feat_half), jnp.float32)
    first_slot, last_slot = slot_bounds(
        tile_src, 0, my_count, start_row, start_row + clusters_here * lax.axis_size("rows")
    )
    summed = lax.psum_scatter(
        sweep_slots(
            first_slot,
            last_slot,
            lambda carried, slot_ids, is_valid: spread_products(
                carried, adj_tiles, tile_src, tile_dst, slot_ids, is_valid, grad_agg
            ),
            totals,
        ),
        "rows",
        scatter_dimension=0,
        tiled=True,
    )
    grad_features = (summed * live_node).reshape(node_rows, feat_half).astype(jnp.bfloat16)
    return (hidden, grad_weight, grad_bias, grad_features)


def solution(mesh):
    return jax.shard_map(
        local,
        mesh=mesh,
        in_specs=(
            P("rows", "cols"),
            P("rows", None, None),
            P("rows"),
            P("rows"),
            P("rows"),
            P("rows"),
            P(None, "cols"),
            P("cols"),
            P("rows", "cols"),
        ),
        out_specs=(P("rows", "cols"), P(None, "cols"), P("cols"), P("rows", "cols")),
        check_vma=False,
    )
```

profile of v0, /device:TPU:1, one launch (start us, length us, event | category | flops | bytes accessed | tf_op | source)
XLA Modules:
  0.0 1831.6 jit_solution(9324555501634384926)
XLA Ops:
  10.1 1.4 fusion.8
  12.8 216.8 %all-gather.2.cloned.1.call-done = bf16[256,128,64]{1,2,0:T(8,128)(2,1)} async-done(((bf16[2,128,64]{1,2,0:T(8,128)(2,1)}), bf16[256,128,64]{1,2,0:T(8,128)(2,1)}) %all-gather.2.cloned.1.call-update) | async-done | bytes 4194320 | tf_op jit(solution)/shard_map/all_gather | solution.py:67
  229.6 8.4 copy.27
  238.1 33.4 %while.20 = (s32[]{:T(128)}, f32[2,128,64]{1,2,0:T(8,128)S(1)}, s32[]{:T(128)}, s32[]{:T(128)}, s32[]{:T(128)}, /*index=5*/s32[96]{0:T(128)S(1)}, bf16[96,128,12...) while((s32[]{:T(128)}, f32[2,128,64]{1,2,0:T(8,128)S(1)}, ...), condition=%wide.region_4.5_spmd, body=%wide.region_2.4_spmd.sunk | while | flops 33687796 | bytes 4465809 | solution.py:18
  240.8 4.0 gather_fusion.3
  244.8 2.5 gather_fusion.1
  251.9 4.0 gather_fusion.3
  255.9 2.5 gather_fusion.1
  263.0 4.0 gather_fusion.3
  267.0 2.5 gather_fusion.1
  271.5 4.9 all_gather.7
  279.0 48.3 %reduce-scatter.3.cloned.1.call-done = f32[256,64]{0,1:T(8,128)} async-done(((f32[256,128]{0,1:T(8,128)}), f32[256,64]{0,1:T(8,128)}) %reduce-scatter.3.cloned.1.call-update) | async-done | bytes 65552 | tf_op jit(solution)/shard_map/reduce_scatter | solution.py:101
  328.3 4.3 broadcast_in_dim.17
  332.6 26.9 %while.21 = (s32[]{:T(128)}, f32[256,128,64]{1,2,0:T(8,128)}, s32[]{:T(128)}, s32[]{:T(128)}, s32[]{:T(128)}, /*index=5*/s32[96]{0:T(128)S(1)}, bf16[96,128,128]...) while((s32[]{:T(128)}, f32[256,128,64]{1,2,0:T(8,128)}, ...), condition=%wide.region_11.12_spmd, body=%wide.region_9.11_spmd.sunk | while | flops 33687780 | bytes 4465809 | solution.py:18
  335.9 2.5 gather_fusion.5
  338.8 2.8 scatter_fusion.1
  344.9 2.5 gather_fusion.5
  347.8 2.7 scatter_fusion.1
  353.9 2.5 gather_fusion.5
  356.7 2.8 scatter_fusion.1
  359.5 303.3 %psum.15 = f32[128]{0:T(128)S(1)} all-reduce(f32[128]{0:T(128)S(1)} %get-tuple-element.194), channel_id=1, replica_groups=mesh['rows'=128,'cols'=2] {'rows'}, use_global_device_ids=true, to_apply=%region_7.8 | all-reduce | flops 128 | bytes 1024 | tf_op jit(solution)/shard_map/psum | solution.py:93
  663.3 591.1 %all-reduce.2.cloned.1.call-done = f32[128,128]{1,0:T(8,128)} async-done(((f32[128,128]{1,0:T(8,128)}), f32[128,128]{1,0:T(8,128)}) %all-reduce.2.cloned.1.call-update) | async-done | bytes 65552 | tf_op jit(solution)/shard_map/psum | solution.py:93
  1254.4 1.5 broadcast_multiply_fusion
  1255.9 567.7 %reduce-scatter.5.cloned.1.call-done = f32[2,128,64]{1,2,0:T(8,128)} async-done(((f32[256,128,64]{1,2,0:T(8,128)}), f32[2,128,64]{1,2,0:T(8,128)}) %reduce-scatter.5.cloned.1.call-update) | async-done | bytes 65552 | tf_op jit(solution)/shard_map/reduce_scatter | solution.py:110
  (86 shorter events, 28.5 us)
Async XLA Ops:
  7.2 269.2 %copy-start = (bf16[128,128]{1,0:T(8,128)(2,1)S(1)}, bf16[128,128]{1,0:T(8,128)(2,1)}, u32[]{:S(2)}) copy-start(bf16[128,128]{1,0:T(8,128)(2,1)} %param.19) | copy-start | bytes 98308
  7.2 230.8 %copy-start.1 = (s32[96]{0:T(128)S(1)}, s32[96]{0:T(128)}, u32[]{:S(2)}) copy-start(s32[96]{0:T(128)} %param.15) | copy-start | bytes 1156
  7.2 230.8 %copy-start.2 = (s32[96]{0:T(128)S(1)}, s32[96]{0:T(128)}, u32[]{:S(2)}) copy-start(s32[96]{0:T(128)} %param.16) | copy-start | bytes 1156
  7.2 222.4 %all-gather.2.cloned.1.call-start = ((), (), s32[]{:S(2)}) async-start(), calls=%async_computation.2 | async-start | bytes 4227072 | tf_op jit(solution)/shard_map/all_gather | solution.py:67
  9.4 317.9 %reduce-scatter.3.cloned.1.call-start = ((), (), s32[]{:S(2)}) async-start(), calls=%async_computation.4 | async-start | bytes 196608 | tf_op jit(solution)/shard_map/reduce_scatter | solution.py:101
  238.0 38.4 %copy-start.3 = (bf16[256,128]{1,0:T(8,128)(2,1)S(1)}, bf16[256,128]{1,0:T(8,128)(2,1)}, u32[]{:S(2)}) copy-start(bf16[256,128]{1,0:T(8,128)(2,1)} %param.21) | copy-start | bytes 196612
  238.0 38.4 %copy-start.4 = (f32[128]{0:T(128)S(1)}, f32[128]{0:T(128)}, u32[]{:S(2)}) copy-start(f32[128]{0:T(128)} %param.20) | copy-start | bytes 1540
  278.1 976.3 %all-reduce.2.cloned.1.call-start = ((), (), s32[]{:S(2)}) async-start(), calls=%async_computation.3 | async-start | bytes 131072 | tf_op jit(solution)/shard_map/psum | solution.py:93
  279.0 1544.6 %reduce-scatter.5.cloned.1.call-start = ((), (), s32[]{:S(2)}) async-start(), calls=%async_computation.5 | async-start | bytes 8454144 | tf_op jit(solution)/shard_map/reduce_scatter | solution.py:110
Sparse Core Ops, SparseCore 0:
  10.5 219.1 all-gather.1
  278.2 49.0 reduce-scatter.2
  330.5 923.8 all-reduce.1
  1256.9 566.6 reduce-scatter.4
where the time goes:
time: 1840 us; the launch traced here: 1830 us
  waiting for transfers between devices  1420 us (77%)
  blocking collectives  308 us (17%)
  local copies, waits for them, and re-layouts  52.1 us (3%)
  other arithmetic  22.5 us (1%)
    psum x1, waiting for transfers between devices, local(): weight_total, bias_total = lax.psum((weight_term, bias_term), 'rows')  591 us
    reduce_scatter x1, waiting for transfers between devices, local(): lax.psum_scatter(sweep_slots(first_slot, last_slot, lambda carried, slot_...  568 us
    psum x1, blocking collectives, local(): weight_total, bias_total = lax.psum((weight_term, bias_term), 'rows')  303 us
    all_gather x1, waiting for transfers between devices, local(): whole_rows = lax.all_gather(masked, 'rows', axis=0, tiled=True)  217 us
    reduce_scatter x1, waiting for transfers between devices, local(): lax.psum_scatter(partial_value, 'cols', scatter_dimension=1, tiled=True)  48.3 us
  transfers between devices with their start and end apart: 4, of which 4 were waited for; matrix products, arithmetic and copies ran while one was open for 2% of the time, Pallas kernels for 0%

commit v1 on v0

v1 whole, which is shorter than its diff:
```python
import functools
import math

import jax
import jax.numpy as jnp
from jax import lax
from jax.experimental import pallas as pl
from jax.experimental.pallas import tpu as pltpu
from jax.sharding import PartitionSpec as P

F32 = jnp.float32
BF16 = jnp.bfloat16
MESH = pl.DeviceIdType.MESH


def flip_bits(index, mask):
    out = index
    bit = 1
    while bit <= mask:
        if mask & bit:
            out = out + bit - 2 * bit * ((index // bit) % 2)
        bit *= 2
    return out


def layer_kernel(
    plan,
    src_ref,
    dst_ref,
    count_ref,
    size_ref,
    feat_hbm,
    tiles_hbm,
    weight_hbm,
    bias_hbm,
    gout_hbm,
    hidden_ref,
    gw_ref,
    gb_ref,
    gf_ref,
    feat,
    tiles,
    weights,
    biases,
    gouts,
    packed,
    sums,
    dense,
    agg_own,
    agg_other,
    stage,
    fold_in,
    fold_mid,
    fold_all,
    give,
    take,
    own_back,
    load_sem,
    x_send,
    x_recv,
    p_send,
    p_recv,
    c_send,
    c_recv,
    r1_send,
    r1_recv,
    r2_send,
    r2_recv,
    r3_send,
    r3_recv,
):
    near, wide, deep, scale = plan
    levels = len(near)
    wide_count, deep_count = len(wide), len(deep)
    me = lax.axis_index("rows")
    col = lax.axis_index("cols")
    slots = tiles.shape[0]
    tall = tiles.shape[1]

    def remote(src, dst, send, recv, mask):
        who = {"cols": 1 - col} if mask is None else {"rows": flip_bits(me, mask)}
        return pltpu.make_async_remote_copy(
            src_ref=src,
            dst_ref=dst,
            send_sem=send,
            recv_sem=recv,
            device_id=who,
            device_id_type=MESH,
        )

    loads = [
        pltpu.make_async_copy(feat_hbm, feat, load_sem.at[0]),
        pltpu.make_async_copy(weight_hbm, weights.at[0], load_sem.at[1]),
        pltpu.make_async_copy(bias_hbm, biases.at[0], load_sem.at[2]),
        pltpu.make_async_copy(gout_hbm, gouts.at[0], load_sem.at[3]),
        pltpu.make_async_copy(tiles_hbm, tiles, load_sem.at[4]),
    ]
    for load in loads:
        load.start()

    peers = sorted(set(near) | set(wide[1:]) | set(deep[1:]))
    barrier = pltpu.get_barrier_semaphore()
    for mask in peers:
        pl.semaphore_signal(
            barrier, inc=1, device_id={"rows": flip_bits(me, mask)}, device_id_type=MESH
        )
    pl.semaphore_signal(barrier, inc=1, device_id={"cols": 1 - col}, device_id_type=MESH)

    lanes = lax.broadcasted_iota(jnp.int32, (tall, 2 * feat.shape[1]), 1)
    left = lanes < feat.shape[1]
    node = lax.broadcasted_iota(jnp.int32, (tall, tall), 0)
    live = [(node < size_ref[c]).astype(F32) for c in range(2)]
    half = feat.shape[1]

    loads[0].wait()
    pair = jnp.concatenate([feat[:tall, :], feat[tall:, :]], axis=1).astype(F32)
    packed[levels] = jnp.where(left, pair * live[0], pair * live[1]).astype(BF16)

    pl.semaphore_wait(barrier, len(peers) + 1)

    feature_copies = [
        remote(packed.at[levels], packed.at[k], x_send.at[k], x_recv.at[k], near[k])
        for k in range(levels)
    ]
    for copy in feature_copies[::-1]:
        copy.start()
    side_copies = [
        remote(weight_hbm, weights.at[1], p_send.at[0], p_recv.at[0], None),
        remote(bias_hbm, biases.at[1], p_send.at[1], p_recv.at[1], None),
        remote(gout_hbm, gouts.at[1], p_send.at[2], p_recv.at[2], None),
    ]
    for copy in side_copies:
        copy.start()

    clusters = []
    for k in range(levels + 1):
        group = flip_bits(me, near[k]) if k < levels else me
        clusters += [group * 2, group * 2 + 1]
    count = count_ref[0]
    for load in loads[1:]:
        load.wait()

    def one_tile(t, carried):
        first, second, prev, lasts = carried
        src = src_ref[t]
        used = t < count
        keep = (src == prev) & used
        to_second = dst_ref[t] == 1
        tile = tiles[t].astype(F32)
        zero = jnp.zeros_like(tile)
        first = jnp.where(keep, first, zero) + jnp.where(used & (~to_second), tile, zero)
        second = jnp.where(keep, second, zero) + jnp.where(used & to_second, tile, zero)
        sums[0, t] = first.astype(BF16)
        sums[1, t] = second.astype(BF16)
        lasts = tuple(
            jnp.where(used & (src == cluster), t, last)
            for last, cluster in zip(lasts, clusters)
        )
        return first, second, src, lasts

    blank = jnp.zeros((tall, tall), F32)
    lasts = lax.fori_loop(
        0,
        slots,
        one_tile,
        (blank, blank, jnp.int32(-1), tuple(jnp.int32(-1) for _ in clusters)),
    )[3]
    for j, last in enumerate(lasts):
        at = jnp.maximum(last, 0)
        for d in range(2):
            block = sums[d, at]
            dense[j // 2, d * tall : (d + 1) * tall, (j % 2) * tall : (j % 2 + 1) * tall] = (
                jnp.where(last >= 0, block, jnp.zeros_like(block))
            )

    total = None
    for k in [levels] + list(range(levels)):
        if k < levels:
            feature_copies[k].wait_recv()
        block = packed[k]
        none = jnp.zeros_like(block)
        rows = jnp.concatenate(
            [jnp.where(left, block, none), jnp.where(left, none, block)], axis=0
        )
        term = jnp.dot(dense[k], rows, preferred_element_type=F32)
        total = term if total is None else total + term
    total = total + pltpu.roll(total, half, 1)
    agg_own[...] = jnp.where(left, total[:tall], total[tall:]).astype(BF16)
    agg_copy = remote(agg_own, agg_other, p_send.at[3], p_recv.at[3], None)
    agg_copy.start()
    for copy in side_copies:
        copy.wait_recv()
    agg_copy.wait_recv()

    mine, other = agg_own[...].astype(F32), agg_other[...].astype(F32)
    low = jnp.where(col == 0, mine, other)
    high = jnp.where(col == 0, other, mine)
    agg = jnp.concatenate(
        [
            jnp.where(left, low, pltpu.roll(high, half, 1)),
            jnp.where(left, pltpu.roll(low, half, 1), high),
        ],
        axis=0,
    ).astype(BF16)
    live_all = jnp.concatenate(live, axis=0)
    grads = []
    for side in range(2):
        pre = jnp.dot(agg, weights[side], preferred_element_type=F32) + biases[side]
        gate = jax.nn.sigmoid(pre)
        if side == 0:
            hidden_ref[...] = (pre * gate * live_all).astype(BF16)
        grads.append(
            (
                gouts[side].astype(F32) * gate * (1.0 + pre * (1.0 - gate)) * live_all
            ).astype(BF16)
        )

    by_rows = (((0,), (0,)), ((), ()))
    grad_weight = lax.dot_general(agg, grads[0], by_rows, preferred_element_type=F32)
    chunk = grad_weight.shape[0] // wide_count
    grad_bias = jnp.sum(grads[0].astype(F32), axis=0, keepdims=True)
    stage[:, :chunk, :] = grad_weight.reshape(wide_count, chunk, grad_weight.shape[1])
    stage[:, chunk:, :] = jnp.broadcast_to(
        grad_bias[None], (wide_count, stage.shape[1] - chunk, grad_weight.shape[1])
    )

    def place(index, masks):
        out, bit = 0, 1
        while bit < len(masks):
            out = out + bit * ((index // masks[bit]) % 2)
            bit *= 2
        return out

    my_wide, my_deep = place(me, wide), place(me, deep)
    scatter_copies = [
        remote(
            stage.at[place(flip_bits(me, wide[m]), wide)],
            fold_in.at[my_wide],
            r1_send.at[m],
            r1_recv.at[m],
            wide[m],
        )
        for m in range(1, wide_count)
    ]
    for copy in scatter_copies:
        copy.start()
    fold_in[my_wide] = stage[my_wide]

    own_rows = pl.ds(pl.multiple_of(col * half, half), half)
    by_lanes = (((1,), (1,)), ((), ()))
    grad_agg = sum(
        lax.dot_general(
            weights[side, own_rows, :], grads[side], by_lanes, preferred_element_type=F32
        )
        for side in range(2)
    ).astype(BF16)
    back_copies = [
        remote(give.at[k], take.at[k], c_send.at[k], c_recv.at[k], near[k])
        for k in range(levels)
    ]
    for k in range(levels - 1, -1, -1):
        give[k] = jnp.dot(grad_agg, dense[k], preferred_element_type=F32).astype(BF16)
        back_copies[k].start()
    own_back[...] = jnp.dot(grad_agg, dense[levels], preferred_element_type=F32)

    for m in range(1, wide_count):
        remote(
            stage.at[0],
            fold_in.at[place(flip_bits(me, wide[m]), wide)],
            r1_send.at[m],
            r1_recv.at[m],
            wide[m],
        ).wait_recv()
    part = fold_in[0]
    for m in range(1, wide_count):
        part = part + fold_in[m]
    fold_mid[my_deep] = part
    deep_copies = [
        remote(
            fold_mid.at[my_deep], fold_mid.at[my_deep], r2_send.at[m], r2_recv.at[m], deep[m]
        )
        for m in range(1, deep_count)
    ]
    for copy in deep_copies:
        copy.start()

    back = own_back[...]
    for k in range(levels):
        back_copies[k].wait_recv()
        back = back + take[k].astype(F32)
    node_lane = lax.broadcasted_iota(jnp.int32, (half, tall), 1)
    for c in range(2):
        piece = back[:, c * tall : (c + 1) * tall]
        piece = jnp.where(node_lane < size_ref[c], piece, jnp.zeros_like(piece))
        gf_ref[c * tall : (c + 1) * tall, :] = piece.T.astype(BF16)

    for m in range(1, deep_count):
        remote(
            fold_mid.at[my_deep],
            fold_mid.at[place(flip_bits(me, deep[m]), deep)],
            r2_send.at[m],
            r2_recv.at[m],
            deep[m],
        ).wait_recv()
    part = fold_mid[0]
    for m in range(1, deep_count):
        part = part + fold_mid[m]
    part = part * scale
    gb_ref[...] = part[chunk : chunk + 1, :]
    fold_all[my_wide] = part[:chunk]
    gather_copies = [
        remote(
            fold_all.at[my_wide], fold_all.at[my_wide], r3_send.at[m], r3_recv.at[m], wide[m]
        )
        for m in range(1, wide_count)
    ]
    for copy in gather_copies:
        copy.start()
    for m in range(1, wide_count):
        remote(
            fold_all.at[my_wide],
            fold_all.at[place(flip_bits(me, wide[m]), wide)],
            r3_send.at[m],
            r3_recv.at[m],
            wide[m],
        ).wait_recv()
    gw_ref[...] = fold_all[...].reshape(gw_ref.shape)

    for copy in (
        feature_copies
        + side_copies
        + [agg_copy]
        + scatter_copies
        + back_copies
        + deep_copies
        + gather_copies
    ):
        copy.wait_send()


def group_masks(bits):
    return [
        sum(1 << bit for place, bit in enumerate(bits) if m >> place & 1)
        for m in range(1 << len(bits))
    ]


def solution(mesh):
    row_groups = mesh.shape["rows"]
    levels = row_groups.bit_length() - 1
    deep_bits = [bit for bit in range(levels) if 1 <= bit <= (3 if levels > 4 else 1)]
    wide_bits = [bit for bit in range(levels) if bit not in deep_bits]
    near = [1 << bit for bit in range(levels)]
    wide, deep = group_masks(wide_bits), group_masks(deep_bits)

    def local(
        features, adj_tiles, tile_src, tile_dst, tile_count, cluster_size, weight, bias, grad_out
    ):
        slots, tall, _ = adj_tiles.shape
        nodes, half = features.shape
        wide_feat, units = weight.shape
        chunk = wide_feat // len(wide)
        dma = pltpu.SemaphoreType.DMA
        plan = (near, wide, deep, 1.0 / math.sqrt(nodes * row_groups))
        smem = pl.BlockSpec(memory_space=pltpu.SMEM)
        vmem = pl.BlockSpec(memory_space=pltpu.VMEM)
        hbm = pl.BlockSpec(memory_space=pltpu.HBM)
        hidden, grad_weight, grad_bias, grad_features = pl.pallas_call(
            functools.partial(layer_kernel, plan),
            out_shape=(
                jax.ShapeDtypeStruct((nodes, units), BF16),
                jax.ShapeDtypeStruct((wide_feat, units), F32),
                jax.ShapeDtypeStruct((1, units), F32),
                jax.ShapeDtypeStruct((nodes, half), BF16),
            ),
            in_specs=[smem] * 4 + [hbm] * 5,
            out_specs=(vmem,) * 4,
            scratch_shapes=[
                pltpu.VMEM((nodes, half), BF16),
                pltpu.VMEM((slots, tall, tall), BF16),
                pltpu.VMEM((2, wide_feat, units), BF16),
                pltpu.VMEM((2, 1, units), F32),
                pltpu.VMEM((2, nodes, units), BF16),
                pltpu.VMEM((levels + 1, tall, 2 * half), BF16),
                pltpu.VMEM((2, slots, tall, tall), BF16),
                pltpu.VMEM((levels + 1, nodes, nodes), BF16),
                pltpu.VMEM((tall, 2 * half), BF16),
                pltpu.VMEM((tall, 2 * half), BF16),
                pltpu.VMEM((len(wide), chunk + 8, units), F32),
                pltpu.VMEM((len(wide), chunk + 8, units), F32),
                pltpu.VMEM((len(deep), chunk + 8, units), F32),
                pltpu.VMEM((len(wide), chunk, units), F32),
                pltpu.VMEM((levels, half, nodes), BF16),
                pltpu.VMEM((levels, half, nodes), BF16),
                pltpu.VMEM((half, nodes), F32),
                dma((5,)),
                dma((levels,)),
                dma((levels,)),
                dma((4,)),
                dma((4,)),
                dma((levels,)),
                dma((levels,)),
                dma((len(wide),)),
                dma((len(wide),)),
                dma((len(deep),)),
                dma((len(deep),)),
                dma((len(wide),)),
                dma((len(wide),)),
            ],
            compiler_params=pltpu.CompilerParams(
                collective_id=0, has_side_effects=True, vmem_limit_bytes=40 * 1024 * 1024
            ),
            name="graph_layer",
        )(
            tile_src,
            tile_dst,
            tile_count,
            cluster_size,
            features,
            adj_tiles,
            weight,
            bias.reshape(1, units),
            grad_out,
        )
        return hidden, grad_weight, grad_bias.reshape(units), grad_features

    return jax.shard_map(
        local,
        mesh=mesh,
        in_specs=(
            P("rows", "cols"),
            P("rows", None, None),
            P("rows"),
            P("rows"),
            P("rows"),
            P("rows"),
            P(None, "cols"),
            P("cols"),
            P("rows", "cols"),
        ),
        out_specs=(P("rows", "cols"), P(None, "cols"), P("cols"), P("rows", "cols")),
        check_vma=False,
    )
```

time: 1840 us -> 47.6 us (0.03)
  waiting for transfers between devices: 1420 us -> 0 us
  blocking collectives: 308 us -> 0 us
  local copies, waits for them, and re-layouts: 52.1 us -> 9.46 us
  Pallas kernels: 0 us -> 36.5 us
  other arithmetic: 22.5 us -> 0 us
    reduce_scatter x2 -> x0, waiting for transfers between devices: 616 us -> none  [the longest x1 568 us: local(): lax.psum_scatter(sweep_slots(first_slot, last_slot, lambda carried, slot_...]
    psum x1 -> x0, waiting for transfers between devices: 591 us -> none  [local(): weight_total, bias_total = lax.psum((weight_term, bias_term), 'rows')]
    psum x1 -> x0, blocking collectives: 303 us -> none  [local(): weight_total, bias_total = lax.psum((weight_term, bias_term), 'rows')]
    all_gather x1 -> x0, waiting for transfers between devices: 217 us -> none  [local(): whole_rows = lax.all_gather(masked, 'rows', axis=0, tiled=True)]
    gather x24 -> x0, local copies, waits for them, and re-layouts: 37.2 us -> none  [the longest x3 12.1 us: gather_products(): row_table[from_rows]]
    pallas_call x0 -> x1, Pallas kernels: none -> 36.5 us  [local(): pl.pallas_call(functools.partial(layer_kernel, plan), out_shape=(jax.Shap...]
  transfers between devices with their start and end apart: 4 -> 0, of which waited for: 4 -> 0; matrix products, arithmetic and copies ran while one was open for 2% -> 0% of each run, Pallas kernels for 0% -> 0%
where the time goes in v1:
time: 47.6 us; the launch traced here: 47.2 us
  Pallas kernels  36.5 us (77%)
  local copies, waits for them, and re-layouts  9.46 us (20%)
  between operations  1.3 us (3%)
    pallas_call x1, Pallas kernels, local(): pl.pallas_call(functools.partial(layer_kernel, plan), out_shape=(jax.Shap...  36.5 us
    unnamed x19, local copies, waits for them, and re-layouts  9.46 us

profile of v1, /device:TPU:1, one launch (start us, length us, event | category | flops | bytes accessed | tf_op | source)
XLA Modules:
  0.0 47.2 jit_solution(6075764178912022533)
XLA Ops:
  1.3 0.9 %copy.13.feat_hbm = bf16[256,64]{1,0:T(8,128)(2,1)S(1)} copy(bf16[256,64]{0,1:T(8,128)(2,1)} %param.9) | data formatting | bytes 65536 | tf_op args[0]
  2.2 0.0 copy-start
  2.2 1.9 %copy-done = bf16[96,128,128]{2,1,0:T(8,128)(2,1)S(1)} copy-done((bf16[96,128,128]{2,1,0:T(8,128)(2,1)S(1)}, bf16[96,128,128]{2,1,0:T(8,128)(2,1)}, u32[]{:S(2)}) %copy-start) | copy-done | bytes 3145752
  4.0 0.0 copy-start.1
  4.0 0.8 %copy-done.1 = bf16[256,128]{1,0:T(8,128)(2,1)S(1)} copy-done((bf16[256,128]{1,0:T(8,128)(2,1)S(1)}, bf16[256,128]{1,0:T(8,128)(2,1)}, u32[]{:S(2)}) %copy-start.1) | copy-done | bytes 65560
  4.9 0.0 copy-start.2
  4.9 0.8 %copy-done.2 = bf16[128,128]{1,0:T(8,128)(2,1)S(1)} copy-done((bf16[128,128]{1,0:T(8,128)(2,1)S(1)}, bf16[128,128]{1,0:T(8,128)(2,1)}, u32[]{:S(2)}) %copy-start.2) | copy-done | bytes 32792
  5.6 0.0 copy-start.3
  5.6 0.7 %copy-done.3 = s32[96]{0:T(128)S(1)} copy-done((s32[96]{0:T(128)S(1)}, s32[96]{0:T(128)}, u32[]{:S(2)}) %copy-start.3) | copy-done | bytes 408
  6.3 0.0 copy-start.4
  6.3 0.7 %copy-done.4 = s32[96]{0:T(128)S(1)} copy-done((s32[96]{0:T(128)S(1)}, s32[96]{0:T(128)}, u32[]{:S(2)}) %copy-start.4) | copy-done | bytes 408
  7.0 0.0 copy-start.5
  7.0 0.7 %copy-done.5 = s32[2]{0:T(128)S(1)} copy-done((s32[2]{0:T(128)S(1)}, s32[2]{0:T(128)}, u32[]{:S(2)}) %copy-start.5) | copy-done | bytes 32
  7.6 0.0 copy-start.6
  7.6 0.7 %copy-done.6 = f32[128]{0:T(128)S(1)} copy-done((f32[128]{0:T(128)S(1)}, f32[128]{0:T(128)}, u32[]{:S(2)}) %copy-start.6) | copy-done | bytes 536
  8.3 36.5 %graph_layer.1 = (bf16[256,128]{1,0:T(8,128)(2,1)S(1)}, f32[128,128]{1,0:T(8,128)S(1)}, f32[1,128]{1,0:T(1,128)S(1)}, bf16[256,64]{1,0:T(8,128)(2,1)S(1)}) custom-call(s32[96]{0:T(128)S(1)} %copy-done.3, s32[96]{0:T(128)S(1)} %copy-done.4, s32[1]{0:T(128)S(6)} %copy.18.count_ref, s32[2]{0:T(128)S(1)} %copy-done.5, bf16[256,64]{1,0:T(8,128)(2,1)S(1)} %copy.13.feat_hbm, ...), custom_call_target="tpu_custom_call" | custom-call | tf_op jit(solution)/shard_map/graph_layer/pallas_call | solution.py:368
  44.7 0.7 %copy.14 = bf16[256,64]{0,1:T(8,128)(2,1)} copy(bf16[256,64]{1,0:T(8,128)(2,1)S(1)} %get-tuple-element.15) | data formatting | bytes 65536
  45.4 0.6 %copy.19 = bf16[256,128]{1,0:T(8,128)(2,1)} copy(bf16[256,128]{1,0:T(8,128)(2,1)S(1)} %get-tuple-element.20) | data formatting | bytes 131072
  46.1 0.6 %copy.20 = f32[128,128]{1,0:T(8,128)} copy(f32[128,128]{1,0:T(8,128)S(1)} %get-tuple-element.21) | data formatting | bytes 131072
  46.7 0.5 %copy.21 = f32[128]{0:T(128)} copy(f32[128]{0:T(128)S(1)} %bitcast.3) | data formatting | bytes 1024
Async XLA Ops:
  2.2 1.9 %copy-start = (bf16[96,128,128]{2,1,0:T(8,128)(2,1)S(1)}, bf16[96,128,128]{2,1,0:T(8,128)(2,1)}, u32[]{:S(2)}) copy-start(bf16[96,128,128]{2,1,0:T(8,128)(2,1)} %tiles_hbm.1) | copy-start | bytes 9437188
  4.0 0.8 %copy-start.1 = (bf16[256,128]{1,0:T(8,128)(2,1)S(1)}, bf16[256,128]{1,0:T(8,128)(2,1)}, u32[]{:S(2)}) copy-start(bf16[256,128]{1,0:T(8,128)(2,1)} %gout_hbm.1) | copy-start | bytes 196612
  4.9 0.8 %copy-start.2 = (bf16[128,128]{1,0:T(8,128)(2,1)S(1)}, bf16[128,128]{1,0:T(8,128)(2,1)}, u32[]{:S(2)}) copy-start(bf16[128,128]{1,0:T(8,128)(2,1)} %weight_hbm.1) | copy-start | bytes 98308
  5.6 0.7 %copy-start.3 = (s32[96]{0:T(128)S(1)}, s32[96]{0:T(128)}, u32[]{:S(2)}) copy-start(s32[96]{0:T(128)} %src_ref.1) | copy-start | bytes 1156
  6.3 0.7 %copy-start.4 = (s32[96]{0:T(128)S(1)}, s32[96]{0:T(128)}, u32[]{:S(2)}) copy-start(s32[96]{0:T(128)} %dst_ref.1) | copy-start | bytes 1156
  7.0 0.7 %copy-start.5 = (s32[2]{0:T(128)S(1)}, s32[2]{0:T(128)}, u32[]{:S(2)}) copy-start(s32[2]{0:T(128)} %size_ref.1) | copy-start | bytes 28
  7.6 0.7 %copy-start.6 = (f32[128]{0:T(128)S(1)}, f32[128]{0:T(128)}, u32[]{:S(2)}) copy-start(f32[128]{0:T(128)} %param.16) | copy-start | bytes 1540

commit v2 on v1

v2 whole, which is shorter than its diff:
```python
import functools
import math

import jax
import jax.numpy as jnp
from jax import lax
from jax.experimental import pallas as pl
from jax.experimental.pallas import tpu as pltpu
from jax.sharding import PartitionSpec as P

F32 = jnp.float32
BF16 = jnp.bfloat16
MESH = pl.DeviceIdType.MESH
EARLY = 1


def flip_bits(index, mask):
    out = index
    bit = 1
    while bit <= mask:
        if mask & bit:
            out = out + bit - 2 * bit * ((index // bit) % 2)
        bit *= 2
    return out


def place(index, masks):
    out, bit = 0, 1
    while bit < len(masks):
        out = out + bit * ((index // masks[bit]) % 2)
        bit *= 2
    return out


def layer_kernel(
    plan,
    src_hbm,
    dst_hbm,
    count_ref,
    size_hbm,
    feat_hbm,
    tiles_hbm,
    weight_hbm,
    bias_hbm,
    gout_hbm,
    hidden_ref,
    gw_ref,
    gb_ref,
    gf_ref,
    src_ref,
    dst_ref,
    size_ref,
    feat,
    tiles,
    weights,
    biases,
    gouts,
    packed,
    sums,
    dense,
    agg,
    turned,
    gout_turned,
    bias_turned,
    stage,
    fold_in,
    fold_mid,
    fold_all,
    give,
    take,
    own_back,
    load_sem,
    tile_sem,
    x_send,
    x_recv,
    p_send,
    p_recv,
    c_send,
    c_recv,
    r1_send,
    r1_recv,
    r2_send,
    r2_recv,
    r3_send,
    r3_recv,
):
    near, wide, deep, scale, early = plan
    levels = len(near)
    wide_count, deep_count = len(wide), len(deep)
    me = lax.axis_index("rows")
    col = lax.axis_index("cols")
    slots, tall, _ = tiles.shape
    half, nodes = feat.shape
    parts = tile_sem.shape[0]
    part_slots = slots // parts

    def remote(src, dst, send, recv, mask):
        who = {"cols": 1 - col} if mask is None else {"rows": flip_bits(me, mask)}
        return pltpu.make_async_remote_copy(
            src_ref=src,
            dst_ref=dst,
            send_sem=send,
            recv_sem=recv,
            device_id=who,
            device_id_type=MESH,
        )

    peers = sorted(set(near) | set(wide[1:]) | set(deep[1:]))
    barrier = pltpu.get_barrier_semaphore()
    for mask in peers:
        pl.semaphore_signal(
            barrier, inc=1, device_id={"rows": flip_bits(me, mask)}, device_id_type=MESH
        )
    pl.semaphore_signal(barrier, inc=1, device_id={"cols": 1 - col}, device_id_type=MESH)

    loads = [
        pltpu.make_async_copy(here, there, load_sem.at[i])
        for i, (here, there) in enumerate(
            [
                (size_hbm, size_ref),
                (feat_hbm, feat),
                (src_hbm, src_ref),
                (dst_hbm, dst_ref),
                (weight_hbm, weights.at[0]),
                (bias_hbm, biases.at[0]),
                (gout_hbm, gouts.at[0]),
            ]
        )
    ]
    tile_loads = [
        pltpu.make_async_copy(
            tiles_hbm.at[pl.ds(i * part_slots, part_slots)],
            tiles.at[pl.ds(i * part_slots, part_slots)],
            tile_sem.at[i],
        )
        for i in range(parts)
    ]
    for load in loads + tile_loads:
        load.start()

    loads[0].wait()
    loads[1].wait()
    node_lane = lax.broadcasted_iota(jnp.int32, (half, nodes), 1)
    live = node_lane < jnp.where(node_lane < tall, size_ref[0], size_ref[1] + tall)
    packed[levels] = jnp.where(live, feat[...].astype(F32), 0.0).astype(BF16)

    clusters = []
    for k in range(levels + 1):
        group = flip_bits(me, near[k]) if k < levels else me
        clusters += [group * 2, group * 2 + 1]
    for load in loads[2:4]:
        load.wait()
    count = count_ref[0]

    def one_tile(t, carried):
        first, second, prev, lasts = carried
        src = src_ref[t]
        used = t < count
        keep = (src == prev) & used
        to_second = dst_ref[t] == 1
        tile = tiles[t].astype(F32)
        zero = jnp.zeros_like(tile)
        first = jnp.where(keep, first, zero) + jnp.where(used & (~to_second), tile, zero)
        second = jnp.where(keep, second, zero) + jnp.where(used & to_second, tile, zero)
        sums[0, t] = first.astype(BF16)
        sums[1, t] = second.astype(BF16)
        lasts = tuple(
            jnp.where(used & (src == cluster), t, last)
            for last, cluster in zip(lasts, clusters)
        )
        return first, second, src, lasts

    blank = jnp.zeros((tall, tall), F32)
    running = (blank, blank, jnp.int32(-1), tuple(jnp.int32(-1) for _ in clusters))
    for i in range(early):
        tile_loads[i].wait()
        running = lax.fori_loop(i * part_slots, (i + 1) * part_slots, one_tile, running)

    pl.semaphore_wait(barrier, len(peers) + 1)

    feature_copies = [
        remote(packed.at[levels], packed.at[k], x_send.at[k], x_recv.at[k], near[k])
        for k in range(levels)
    ]
    for copy in feature_copies[::-1]:
        copy.start()
    side_copies = [
        remote(weight_hbm, weights.at[1], p_send.at[0], p_recv.at[0], None),
        remote(bias_hbm, biases.at[1], p_send.at[1], p_recv.at[1], None),
        remote(gout_hbm, gouts.at[1], p_send.at[2], p_recv.at[2], None),
    ]
    for copy in side_copies:
        copy.start()

    for i in range(early, parts):
        tile_loads[i].wait()
        running = lax.fori_loop(i * part_slots, (i + 1) * part_slots, one_tile, running)
    for j, last in enumerate(running[3]):
        at = jnp.maximum(last, 0)
        for d in range(2):
            block = sums[d, at]
            dense[j // 2, d * tall : (d + 1) * tall, (j % 2) * tall : (j % 2 + 1) * tall] = (
                jnp.where(last >= 0, block, jnp.zeros_like(block))
            )

    def turn(side):
        turned[side] = weights[side].astype(F32).T.astype(BF16)
        gout_turned[side] = gouts[side].astype(F32).T.astype(BF16)
        bias_turned[side] = jnp.broadcast_to(biases[side], (tall, biases.shape[2])).T

    for load in loads[4:]:
        load.wait()
    turn(0)

    by_lanes = (((1,), (1,)), ((), ()))
    total = None
    for k in [levels] + list(range(levels)):
        if k < levels:
            feature_copies[k].wait_recv()
        term = lax.dot_general(packed[k], dense[k], by_lanes, preferred_element_type=F32)
        total = term if total is None else total + term
    own_rows = pl.ds(pl.multiple_of(col * half, half), half)
    agg[own_rows, :] = total.astype(BF16)
    agg_copy = remote(
        agg.at[own_rows, :], agg.at[own_rows, :], p_send.at[3], p_recv.at[3], None
    )
    agg_copy.start()
    for copy in side_copies:
        copy.wait_recv()
    turn(1)
    other_rows = pl.ds(pl.multiple_of((1 - col) * half, half), half)
    remote(
        agg.at[own_rows, :], agg.at[other_rows, :], p_send.at[3], p_recv.at[3], None
    ).wait_recv()

    agg_all = agg[...]
    node_lane = lax.broadcasted_iota(jnp.int32, (turned.shape[1], nodes), 1)
    live_all = node_lane < jnp.where(node_lane < tall, size_ref[0], size_ref[1] + tall)
    grads = []
    hidden = None
    for side in range(2):
        pre = jnp.dot(turned[side], agg_all, preferred_element_type=F32)
        pre = pre + jnp.concatenate([bias_turned[side]] * (nodes // tall), axis=1)
        gate = jax.nn.sigmoid(pre)
        if side == 0:
            hidden = jnp.where(live_all, pre * gate, 0.0)
        grad = gout_turned[side].astype(F32) * gate * (1.0 + pre * (1.0 - gate))
        grads.append(jnp.where(live_all, grad, 0.0).astype(BF16))

    ones = jnp.ones((16, nodes), BF16)
    grad_weight = lax.dot_general(
        jnp.concatenate([agg_all, ones], axis=0),
        grads[0],
        by_lanes,
        preferred_element_type=F32,
    )
    wide_feat, units = gw_ref.shape
    chunk = wide_feat // wide_count
    for j in range(wide_count):
        stage[j, :chunk, :] = grad_weight[j * chunk : (j + 1) * chunk]
        stage[j, chunk:, :] = grad_weight[wide_feat : wide_feat + 8]

    my_wide, my_deep = place(me, wide), place(me, deep)
    scatter_copies = [
        remote(
            stage.at[place(flip_bits(me, wide[m]), wide)],
            fold_in.at[my_wide],
            r1_send.at[m],
            r1_recv.at[m],
            wide[m],
        )
        for m in range(1, wide_count)
    ]
    for copy in scatter_copies:
        copy.start()
    fold_in[my_wide] = stage[my_wide]

    grad_agg = sum(
        jnp.dot(weights[side, own_rows, :], grads[side], preferred_element_type=F32)
        for side in range(2)
    ).astype(BF16)
    back_copies = [
        remote(give.at[k], take.at[k], c_send.at[k], c_recv.at[k], near[k])
        for k in range(levels)
    ]
    for k in range(levels - 1, -1, -1):
        give[k] = jnp.dot(grad_agg, dense[k], preferred_element_type=F32).astype(BF16)
        back_copies[k].start()
    own_back[...] = jnp.dot(grad_agg, dense[levels], preferred_element_type=F32)
    hidden_ref[...] = hidden.T.astype(BF16)

    for m in range(1, wide_count):
        remote(
            stage.at[0],
            fold_in.at[place(flip_bits(me, wide[m]), wide)],
            r1_send.at[m],
            r1_recv.at[m],
            wide[m],
        ).wait_recv()
    part = fold_in[0]
    for m in range(1, wide_count):
        part = part + fold_in[m]
    fold_mid[my_deep] = part
    deep_copies = [
        remote(
            fold_mid.at[my_deep], fold_mid.at[my_deep], r2_send.at[m], r2_recv.at[m], deep[m]
        )
        for m in range(1, deep_count)
    ]
    for copy in deep_copies:
        copy.start()

    back = own_back[...]
    for k in range(levels):
        back_copies[k].wait_recv()
        back = back + take[k].astype(F32)
    gf_ref[...] = jnp.where(live, back, 0.0).astype(BF16)

    for m in range(1, deep_count):
        remote(
            fold_mid.at[my_deep],
            fold_mid.at[place(flip_bits(me, deep[m]), deep)],
            r2_send.at[m],
            r2_recv.at[m],
            deep[m],
        ).wait_recv()
    part = fold_mid[0]
    for m in range(1, deep_count):
        part = part + fold_mid[m]
    part = part * scale
    gb_ref[...] = part[chunk : chunk + 1, :]
    fold_all[my_wide] = part[:chunk]
    gather_copies = [
        remote(
            fold_all.at[my_wide], fold_all.at[my_wide], r3_send.at[m], r3_recv.at[m], wide[m]
        )
        for m in range(1, wide_count)
    ]
    for copy in gather_copies:
        copy.start()
    for m in range(1, wide_count):
        remote(
            fold_all.at[my_wide],
            fold_all.at[place(flip_bits(me, wide[m]), wide)],
            r3_send.at[m],
            r3_recv.at[m],
            wide[m],
        ).wait_recv()
    gw_ref[...] = fold_all[...].reshape(gw_ref.shape)

    for copy in (
        feature_copies
        + side_copies
        + [agg_copy]
        + scatter_copies
        + back_copies
        + deep_copies
        + gather_copies
    ):
        copy.wait_send()


def write_kernel(*refs):
    count = (len(refs) - 1) // 2
    sem = refs[-1]
    copies = [
        pltpu.make_async_copy(refs[i], refs[count + i], sem.at[i]) for i in range(count)
    ]
    for copy in copies:
        copy.start()
    for copy in copies:
        copy.wait()


def group_masks(bits):
    return [
        sum(1 << bit for place, bit in enumerate(bits) if m >> place & 1)
        for m in range(1 << len(bits))
    ]


def solution(mesh):
    row_groups = mesh.shape["rows"]
    levels = row_groups.bit_length() - 1
    deep_bits = [bit for bit in range(levels) if 1 <= bit <= (3 if levels > 4 else 1)]
    wide_bits = [bit for bit in range(levels) if bit not in deep_bits]
    near = [1 << bit for bit in range(levels)]
    wide, deep = group_masks(wide_bits), group_masks(deep_bits)

    def local(
        features, adj_tiles, tile_src, tile_dst, tile_count, cluster_size, weight, bias, grad_out
    ):
        slots, tall, _ = adj_tiles.shape
        nodes, half = features.shape
        wide_feat, units = weight.shape
        chunk = wide_feat // len(wide)
        dma = pltpu.SemaphoreType.DMA
        plan = (near, wide, deep, 1.0 / math.sqrt(nodes * row_groups), EARLY)
        shapes = [
            ((nodes, units), BF16),
            ((wide_feat, units), F32),
            ((1, units), F32),
            ((half, nodes), BF16),
        ]
        inputs = [
            tile_src,
            tile_dst,
            tile_count,
            cluster_size,
            features.T,
            adj_tiles,
            weight,
            bias.reshape(1, units),
            grad_out,
        ]
        results = pl.pallas_call(
            functools.partial(layer_kernel, plan),
            out_shape=tuple(pltpu.VMEM(shape, kind) for shape, kind in shapes),
            in_specs=[
                pl.BlockSpec(memory_space=pltpu.SMEM if x is tile_count else pltpu.HBM)
                for x in inputs
            ],
            out_specs=(pl.BlockSpec(memory_space=pltpu.VMEM),) * len(shapes),
            scratch_shapes=[
                pltpu.SMEM((slots,), jnp.int32),
                pltpu.SMEM((slots,), jnp.int32),
                pltpu.SMEM((2,), jnp.int32),
                pltpu.VMEM((half, nodes), BF16),
                pltpu.VMEM((slots, tall, tall), BF16),
                pltpu.VMEM((2, wide_feat, units), BF16),
                pltpu.VMEM((2, 1, units), F32),
                pltpu.VMEM((2, nodes, units), BF16),
                pltpu.VMEM((levels + 1, half, nodes), BF16),
                pltpu.VMEM((2, slots, tall, tall), BF16),
                pltpu.VMEM((levels + 1, nodes, nodes), BF16),
                pltpu.VMEM((wide_feat, nodes), BF16),
                pltpu.VMEM((2, units, wide_feat), BF16),
                pltpu.VMEM((2, units, nodes), BF16),
                pltpu.VMEM((2, units, tall), F32),
                pltpu.VMEM((len(wide), chunk + 8, units), F32),
                pltpu.VMEM((len(wide), chunk + 8, units), F32),
                pltpu.VMEM((len(deep), chunk + 8, units), F32),
                pltpu.VMEM((len(wide), chunk, units), F32),
                pltpu.VMEM((levels, half, nodes), BF16),
                pltpu.VMEM((levels, half, nodes), BF16),
                pltpu.VMEM((half, nodes), F32),
                dma((7,)),
                dma((4,)),
                dma((levels,)),
                dma((levels,)),
                dma((4,)),
                dma((4,)),
                dma((levels,)),
                dma((levels,)),
                dma((len(wide),)),
                dma((len(wide),)),
                dma((len(deep),)),
                dma((len(deep),)),
                dma((len(wide),)),
                dma((len(wide),)),
            ],
            compiler_params=pltpu.CompilerParams(
                collective_id=0, has_side_effects=True, vmem_limit_bytes=40 * 1024 * 1024
            ),
            name="graph_layer",
        )(
            *[
                x if x is tile_count else pltpu.with_memory_space_constraint(x, pltpu.HBM)
                for x in inputs
            ]
        )
        hidden, grad_weight, grad_bias, grad_features = pl.pallas_call(
            write_kernel,
            out_shape=tuple(pltpu.HBM(shape, kind) for shape, kind in shapes),
            in_specs=[pl.BlockSpec(memory_space=pltpu.VMEM)] * len(shapes),
            out_specs=(pl.BlockSpec(memory_space=pltpu.HBM),) * len(shapes),
            scratch_shapes=[dma((len(shapes),))],
            name="write_results",
        )(*[pltpu.with_memory_space_constraint(x, pltpu.VMEM) for x in results])
        return hidden, grad_weight, grad_bias.reshape(units), grad_features.T

    return jax.shard_map(
        local,
        mesh=mesh,
        in_specs=(
            P("rows", "cols"),
            P("rows", None, None),
            P("rows"),
            P("rows"),
            P("rows"),
            P("rows"),
            P(None, "cols"),
            P("cols"),
            P("rows", "cols"),
        ),
        out_specs=(P("rows", "cols"), P(None, "cols"), P("cols"), P("rows", "cols")),
        check_vma=False,
    )
```

time: 47.6 us -> 37.4 us (0.79)
  local copies, waits for them, and re-layouts: 9.46 us -> 0 us
    unnamed x19 -> x0, local copies, waits for them, and re-layouts: 9.46 us -> none
    pallas_call x1 -> x2, Pallas kernels: 36.5 us -> 36.1 us  [the longest x1 35.4 us: local(): pl.pallas_call(functools.partial(layer_kernel, plan), out_shape=tuple((pl...]
where the time goes in v2:
time: 37.4 us; the launch traced here: 37.3 us
  Pallas kernels  36.1 us (97%)
  between operations  1.29 us (3%)
    pallas_call x1, Pallas kernels, local(): pl.pallas_call(functools.partial(layer_kernel, plan), out_shape=tuple((pl...  35.4 us

profile of v2, /device:TPU:1, one launch (start us, length us, event | category | flops | bytes accessed | tf_op | source)
XLA Modules:
  0.0 37.3 jit_solution(12029312572941516572)
XLA Ops:
  1.3 35.4 %graph_layer.1 = (bf16[256,128]{1,0:T(8,128)(2,1)S(1)}, f32[128,128]{1,0:T(8,128)S(1)}, f32[1,128]{1,0:T(1,128)S(1)}, bf16[64,256]{1,0:T(8,128)(2,1)S(1)}) custom-call(s32[96]{0:T(128)} %src_hbm.1, s32[96]{0:T(128)} %dst_hbm.1, s32[1]{0:T(128)S(6)} %copy.13.count_ref, s32[2]{0:T(128)} %size_hbm.1, bf16[64,256]{1,0:T(8,128)(2,1)} %bitcast.4, ...), custom_call_target="tpu_custom_call" | custom-call | tf_op jit(solution)/shard_map/graph_layer/pallas_call | solution.py:416
  36.6 0.7 %write_results.1 = (bf16[256,128]{1,0:T(8,128)(2,1)}, f32[128,128]{1,0:T(8,128)}, f32[1,128]{1,0:T(1,128)}, bf16[64,256]{1,0:T(8,128)(2,1)}) custom-call(bf16[256,128]{1,0:T(8,128)(2,1)S(1)} %get-tuple-element.12.refs_0_, f32[128,128]{1,0:T(8,128)S(1)} %get-tuple-element.13.refs_1_, f32[1,128]{1,0:T(1,128)S(1)} %get-tuple-element.14.refs_2_, ...), custom_call_target="tpu_custom_call" | custom-call | tf_op jit(solution)/shard_map/write_results/pallas_call | solution.py:472

commit v3 on v2

v3 whole, which is shorter than its diff:
```python
import functools
import math

import jax
import jax.numpy as jnp
from jax import lax
from jax.experimental import pallas as pl
from jax.experimental.pallas import tpu as pltpu
from jax.sharding import PartitionSpec as P

F32 = jnp.float32
BF16 = jnp.bfloat16
MESH = pl.DeviceIdType.MESH
PARTS = 4
MID = jnp.bfloat16
RELAY = 0


class Spot:
    def __init__(self, index, levels):
        self.index = index
        self.levels = levels
        self.bits = [lax.rem(lax.div(index, jnp.int32(1 << b)), jnp.int32(2)) for b in range(levels)]

    def flipped(self, mask):
        out = self.index
        for b in range(self.levels):
            if mask >> b & 1:
                out = out + ((1 << b) - (2 << b) * self.bits[b])
        return out

    def place(self, masks, mask=0):
        out = jnp.int32(0)
        for p in range(len(masks).bit_length() - 1):
            bit = self.bits[masks[1 << p].bit_length() - 1]
            out = out + (1 << p) * (1 - bit if masks[1 << p] & mask else bit)
        return out


def reach(mask):
    z, y, x = mask >> 1 & 7, mask >> 4 & 3, mask >> 6
    far_z = max(min(abs((a ^ z) - a), 8 - abs((a ^ z) - a)) for a in range(8))
    far_y = max(min(abs((a ^ y) - a), 4 - abs((a ^ y) - a)) for a in range(4))
    return far_z + far_y + x


def layer_kernel(
    plan,
    src_hbm,
    dst_hbm,
    count_ref,
    size_hbm,
    feat_hbm,
    tiles_hbm,
    weight_hbm,
    bias_hbm,
    gout_hbm,
    hidden_ref,
    gw_ref,
    gb_ref,
    gf_ref,
    src_ref,
    dst_ref,
    size_ref,
    feat,
    tiles,
    weights,
    biases,
    gouts,
    packed,
    sums,
    dense,
    turned,
    gout_turned,
    part_back,
    part_in,
    stage,
    fold_in,
    fold_mid,
    fold_all,
    bias_in,
    bias_mid,
    give,
    take,
    own_back,
    load_sem,
    tile_sem,
    x_send,
    x_recv,
    y_send,
    y_recv,
    p_send,
    p_recv,
    c_send,
    c_recv,
    r1_send,
    r1_recv,
    r2_send,
    r2_recv,
    r3_send,
    r3_recv,
    b1_send,
    b1_recv,
    b2_send,
    b2_recv,
):
    near, wide, deep, scale = plan
    levels = len(near)
    wide_count, deep_count = len(wide), len(deep)
    me = Spot(lax.axis_index("rows"), levels)
    col = lax.axis_index("cols")
    slots, tall, _ = tiles.shape
    half, nodes = feat.shape
    own_rows = pl.ds(pl.multiple_of(col * half, half), half)
    other_rows = pl.ds(pl.multiple_of((1 - col) * half, half), half)
    relayed = [k for k in range(levels) if reach(near[k]) <= RELAY]
    across = [k for k in range(levels + 1) if k not in relayed]
    far_near = sorted(range(levels), key=lambda k: -reach(near[k]))
    far_wide = sorted(range(1, wide_count), key=lambda m: -reach(wide[m]))
    far_deep = sorted(range(1, deep_count), key=lambda m: -reach(deep[m]))
    parts = tile_sem.shape[0]
    part_slots = slots // parts

    def remote(src, dst, send, recv, mask, crossing=False):
        who = {"rows": me.flipped(mask)} if mask else {}
        if crossing:
            who["cols"] = 1 - col
        return pltpu.make_async_remote_copy(
            src_ref=src,
            dst_ref=dst,
            send_sem=send,
            recv_sem=recv,
            device_id=who,
            device_id_type=MESH,
        )

    peers = [(mask, False) for mask in set(near) | set(wide[1:]) | set(deep[1:])]
    peers += [(near[k] if k < levels else 0, True) for k in across]
    peers.sort(key=lambda peer: -reach(peer[0]) - 2 * peer[1])
    barrier = pltpu.get_barrier_semaphore()
    for mask, crossing in peers:
        who = {"rows": me.flipped(mask)} if mask else {}
        if crossing:
            who["cols"] = 1 - col
        pl.semaphore_signal(barrier, inc=1, device_id=who, device_id_type=MESH)

    loads = [
        pltpu.make_async_copy(here, there, load_sem.at[i])
        for i, (here, there) in enumerate(
            [
                (size_hbm, size_ref),
                (feat_hbm, feat),
                (src_hbm, src_ref),
                (dst_hbm, dst_ref),
                (weight_hbm, weights),
                (bias_hbm, biases),
                (gout_hbm, gouts),
            ]
        )
    ]
    tile_loads = [
        pltpu.make_async_copy(
            tiles_hbm.at[pl.ds(i * part_slots, part_slots)],
            tiles.at[pl.ds(i * part_slots, part_slots)],
            tile_sem.at[i],
        )
        for i in range(parts)
    ]
    for load in loads + tile_loads:
        load.start()

    loads[0].wait()
    loads[1].wait()
    node_lane = lax.broadcasted_iota(jnp.int32, (half, nodes), 1)
    live = node_lane < jnp.where(node_lane < tall, size_ref[0], size_ref[1] + tall)
    packed[levels, own_rows, :] = jnp.where(live, feat[...].astype(F32), 0.0).astype(BF16)

    clusters = []
    for k in range(levels + 1):
        group = me.flipped(near[k]) if k < levels else me.index
        clusters += [group * 2, group * 2 + 1]
    for load in loads[2:4]:
        load.wait()
    count = count_ref[0]

    def one_tile(t, carried):
        first, second, prev, lasts = carried
        src = src_ref[t]
        used = t < count
        keep = (src == prev) & used
        to_second = dst_ref[t] == 1
        tile = tiles[t].astype(F32)
        zero = jnp.zeros_like(tile)
        first = jnp.where(keep, first, zero) + jnp.where(used & (~to_second), tile, zero)
        second = jnp.where(keep, second, zero) + jnp.where(used & to_second, tile, zero)
        sums[0, t] = first.astype(BF16)
        sums[1, t] = second.astype(BF16)
        lasts = tuple(
            jnp.where(used & (src == cluster), t, last)
            for last, cluster in zip(lasts, clusters)
        )
        return first, second, src, lasts

    blank = jnp.zeros((tall, tall), F32)
    running = (blank, blank, jnp.int32(-1), tuple(jnp.int32(-1) for _ in clusters))
    pl.semaphore_wait(barrier, len(peers))

    mine = packed.at[levels, own_rows, :]
    feature_copies = {
        (k, crossing): remote(
            mine,
            packed.at[k, own_rows, :],
            (y_send if crossing else x_send).at[k],
            (y_recv if crossing else x_recv).at[k],
            near[k] if k < levels else 0,
            crossing,
        )
        for crossing in (True, False)
        for k in (across if crossing else range(levels))
    }
    feature_order = sorted(
        feature_copies,
        key=lambda c: -(reach(near[c[0]]) if c[0] < levels else 9) - 2 * c[1],
    )
    for c in feature_order:
        feature_copies[c].start()

    for i in range(parts):
        tile_loads[i].wait()
        running = lax.fori_loop(i * part_slots, (i + 1) * part_slots, one_tile, running)
    theirs = packed.at[levels, other_rows, :]
    relays = [
        remote(theirs, packed.at[k, other_rows, :], y_send.at[k], y_recv.at[k], near[k])
        for k in relayed
    ]
    if relayed:
        remote(
            mine, theirs, y_send.at[levels], y_recv.at[levels], near[0], True
        ).wait_recv()
    for copy in relays:
        copy.start()

    for j, last in enumerate(running[3]):
        at = jnp.maximum(last, 0)
        for d in range(2):
            block = sums[d, at]
            dense[j // 2, d * tall : (d + 1) * tall, (j % 2) * tall : (j % 2 + 1) * tall] = (
                jnp.where(last >= 0, block, jnp.zeros_like(block))
            )

    for load in loads[4:]:
        load.wait()
    turned[...] = weights[...].astype(F32).T.astype(BF16)
    gout_turned[...] = gouts[...].astype(F32).T
    bias_turned = jnp.broadcast_to(biases[...], (tall, biases.shape[1])).T

    by_lanes = (((1,), (1,)), ((), ()))
    total = None
    for k in [levels] + far_near[::-1]:
        if k < levels:
            feature_copies[k, False].wait_recv()
        if k < levels or not relayed:
            remote(
                mine, packed.at[k, other_rows, :], y_send.at[k], y_recv.at[k], near[0], True
            ).wait_recv()
        term = lax.dot_general(packed[k], dense[k], by_lanes, preferred_element_type=F32)
        total = term if total is None else total + term
    agg_all = total.astype(BF16)

    node_lane = lax.broadcasted_iota(jnp.int32, (turned.shape[0], nodes), 1)
    live_all = node_lane < jnp.where(node_lane < tall, size_ref[0], size_ref[1] + tall)
    pre = jnp.dot(turned[...], agg_all, preferred_element_type=F32)
    pre = pre + jnp.concatenate([bias_turned] * (nodes // tall), axis=1)
    gate = jax.nn.sigmoid(pre)
    hidden = jnp.where(live_all, pre * gate, 0.0)
    grad = gout_turned[...] * gate * (1.0 + pre * (1.0 - gate))
    grad = jnp.where(live_all, grad, 0.0).astype(BF16)

    ones = jnp.ones((16, nodes), BF16)
    grad_weight = lax.dot_general(
        jnp.concatenate([agg_all, ones], axis=0),
        grad,
        by_lanes,
        preferred_element_type=F32,
    )
    wide_feat, units = gw_ref.shape
    chunk = wide_feat // wide_count
    for j in range(wide_count):
        stage[j] = grad_weight[j * chunk : (j + 1) * chunk]
    my_wide, my_deep = me.place(wide), me.place(deep)
    bias_in[my_wide] = grad_weight[wide_feat : wide_feat + 1]
    scatter_copies, bias_copies = [], []
    for m in far_wide:
        scatter_copies.append(
            remote(
                stage.at[me.place(wide, wide[m])],
                fold_in.at[my_wide],
                r1_send.at[m],
                r1_recv.at[m],
                wide[m],
            )
        )
        bias_copies.append(
            remote(
                bias_in.at[my_wide],
                bias_in.at[my_wide],
                b1_send.at[m],
                b1_recv.at[m],
                wide[m],
            )
        )
        scatter_copies[-1].start()
        bias_copies[-1].start()
    fold_in[my_wide] = stage[my_wide]

    part_back[...] = jnp.dot(weights[...], grad, preferred_element_type=F32)
    half_copy = remote(
        part_back.at[other_rows, :], part_in, p_send.at[0], p_recv.at[0], 0, True
    )
    half_copy.start()
    hidden_ref[...] = hidden.T.astype(BF16)

    for m in far_wide[::-1]:
        there = me.place(wide, wide[m])
        remote(
            stage.at[0], fold_in.at[there], r1_send.at[m], r1_recv.at[m], wide[m]
        ).wait_recv()
        remote(
            bias_in.at[there], bias_in.at[there], b1_send.at[m], b1_recv.at[m], wide[m]
        ).wait_recv()
    part, bias_part = fold_in[0], bias_in[0]
    for m in range(1, wide_count):
        part, bias_part = part + fold_in[m], bias_part + bias_in[m]
    fold_mid[my_deep] = part.astype(fold_mid.dtype)
    bias_mid[my_deep] = bias_part
    deep_copies = []
    for m in far_deep:
        for fold, send, recv in ((fold_mid, r2_send, r2_recv), (bias_mid, b2_send, b2_recv)):
            deep_copies.append(
                remote(fold.at[my_deep], fold.at[my_deep], send.at[m], recv.at[m], deep[m])
            )
            deep_copies[-1].start()

    half_copy.wait_recv()
    grad_agg = (part_back[own_rows, :] + part_in[...]).astype(BF16)
    back_copies = [
        remote(give.at[k], take.at[k], c_send.at[k], c_recv.at[k], near[k])
        for k in range(levels)
    ]
    for k in far_near[::-1]:
        give[k] = jnp.dot(grad_agg, dense[k], preferred_element_type=F32).astype(BF16)
        back_copies[k].start()
    own_back[...] = jnp.dot(grad_agg, dense[levels], preferred_element_type=F32)

    for m in far_deep[::-1]:
        there = me.place(deep, deep[m])
        for fold, send, recv in ((fold_mid, r2_send, r2_recv), (bias_mid, b2_send, b2_recv)):
            remote(
                fold.at[there], fold.at[there], send.at[m], recv.at[m], deep[m]
            ).wait_recv()
    part, bias_part = fold_mid[0].astype(F32), bias_mid[0]
    for m in range(1, deep_count):
        part, bias_part = part + fold_mid[m].astype(F32), bias_part + bias_mid[m]
    fold_all[my_wide] = part * scale
    gather_copies = [
        remote(
            fold_all.at[my_wide], fold_all.at[my_wide], r3_send.at[m], r3_recv.at[m], wide[m]
        )
        for m in far_wide
    ]
    for copy in gather_copies:
        copy.start()
    gb_ref[...] = bias_part * scale

    back = own_back[...]
    for k in far_near[::-1]:
        back_copies[k].wait_recv()
        back = back + take[k].astype(F32)
    gf_ref[...] = jnp.where(live, back, 0.0).astype(BF16)

    for m in far_wide[::-1]:
        remote(
            fold_all.at[my_wide],
            fold_all.at[me.place(wide, wide[m])],
            r3_send.at[m],
            r3_recv.at[m],
            wide[m],
        ).wait_recv()
    gw_ref[...] = fold_all[...].reshape(gw_ref.shape)

    for copy in (
        list(feature_copies.values())
        + relays
        + scatter_copies
        + bias_copies
        + [half_copy]
        + back_copies
        + deep_copies
        + gather_copies
    ):
        copy.wait_send()


def write_kernel(*refs):
    count = (len(refs) - 1) // 2
    sem = refs[-1]
    copies = [
        pltpu.make_async_copy(refs[i], refs[count + i], sem.at[i]) for i in range(count)
    ]
    for copy in copies:
        copy.start()
    for copy in copies:
        copy.wait()


def group_masks(bits):
    return [
        sum(1 << bit for place, bit in enumerate(bits) if m >> place & 1)
        for m in range(1 << len(bits))
    ]


def solution(mesh):
    row_groups = mesh.shape["rows"]
    levels = row_groups.bit_length() - 1
    wide_bits = [bit for bit in range(levels) if bit in (0, 4, 5)]
    deep_bits = [bit for bit in range(levels) if bit not in wide_bits]
    near = [1 << bit for bit in range(levels)]
    wide, deep = group_masks(wide_bits), group_masks(deep_bits)

    def local(
        features, adj_tiles, tile_src, tile_dst, tile_count, cluster_size, weight, bias, grad_out
    ):
        slots, tall, _ = adj_tiles.shape
        nodes, half = features.shape
        wide_feat, units = weight.shape
        chunk = wide_feat // len(wide)
        dma = pltpu.SemaphoreType.DMA
        plan = (near, wide, deep, 1.0 / math.sqrt(nodes * row_groups))
        shapes = [
            ((nodes, units), BF16),
            ((wide_feat, units), F32),
            ((1, units), F32),
            ((half, nodes), BF16),
        ]
        inputs = [
            tile_src,
            tile_dst,
            tile_count,
            cluster_size,
            features.T,
            adj_tiles,
            weight,
            bias.reshape(1, units),
            grad_out,
        ]
        results = pl.pallas_call(
            functools.partial(layer_kernel, plan),
            out_shape=tuple(pltpu.VMEM(shape, kind) for shape, kind in shapes),
            in_specs=[
                pl.BlockSpec(memory_space=pltpu.SMEM if x is tile_count else pltpu.HBM)
                for x in inputs
            ],
            out_specs=(pl.BlockSpec(memory_space=pltpu.VMEM),) * len(shapes),
            scratch_shapes=[
                pltpu.SMEM((slots,), jnp.int32),
                pltpu.SMEM((slots,), jnp.int32),
                pltpu.SMEM((2,), jnp.int32),
                pltpu.VMEM((half, nodes), BF16),
                pltpu.VMEM((slots, tall, tall), BF16),
                pltpu.VMEM((wide_feat, units), BF16),
                pltpu.VMEM((1, units), F32),
                pltpu.VMEM((nodes, units), BF16),
                pltpu.VMEM((levels + 1, wide_feat, nodes), BF16),
                pltpu.VMEM((2, slots, tall, tall), BF16),
                pltpu.VMEM((levels + 1, nodes, nodes), BF16),
                pltpu.VMEM((units, wide_feat), BF16),
                pltpu.VMEM((units, nodes), F32),
                pltpu.VMEM((wide_feat, nodes), F32),
                pltpu.VMEM((half, nodes), F32),
                pltpu.VMEM((len(wide), chunk, units), F32),
                pltpu.VMEM((len(wide), chunk, units), F32),
                pltpu.VMEM((len(deep), chunk, units), MID),
                pltpu.VMEM((len(wide), chunk, units), F32),
                pltpu.VMEM((len(wide), 1, units), F32),
                pltpu.VMEM((len(deep), 1, units), F32),
                pltpu.VMEM((levels, half, nodes), BF16),
                pltpu.VMEM((levels, half, nodes), BF16),
                pltpu.VMEM((half, nodes), F32),
                dma((7,)),
                dma((PARTS,)),
                dma((levels,)),
                dma((levels,)),
                dma((levels + 1,)),
                dma((levels + 1,)),
                dma((1,)),
                dma((1,)),
                dma((levels,)),
                dma((levels,)),
                dma((len(wide),)),
                dma((len(wide),)),
                dma((len(deep),)),
                dma((len(deep),)),
                dma((len(wide),)),
                dma((len(wide),)),
                dma((len(wide),)),
                dma((len(wide),)),
                dma((len(deep),)),
                dma((len(deep),)),
            ],
            compiler_params=pltpu.CompilerParams(
                collective_id=0, has_side_effects=True, vmem_limit_bytes=40 * 1024 * 1024
            ),
            name="graph_layer",
        )(
            *[
                x if x is tile_count else pltpu.with_memory_space_constraint(x, pltpu.HBM)
                for x in inputs
            ]
        )
        hidden, grad_weight, grad_bias, grad_features = pl.pallas_call(
            write_kernel,
            out_shape=tuple(pltpu.HBM(shape, kind) for shape, kind in shapes),
            in_specs=[pl.BlockSpec(memory_space=pltpu.VMEM)] * len(shapes),
            out_specs=(pl.BlockSpec(memory_space=pltpu.HBM),) * len(shapes),
            scratch_shapes=[dma((len(shapes),))],
            name="write_results",
        )(*[pltpu.with_memory_space_constraint(x, pltpu.VMEM) for x in results])
        return hidden, grad_weight, grad_bias.reshape(units), grad_features.T

    return jax.shard_map(
        local,
        mesh=mesh,
        in_specs=(
            P("rows", "cols"),
            P("rows", None, None),
            P("rows"),
            P("rows"),
            P("rows"),
            P("rows"),
            P(None, "cols"),
            P("cols"),
            P("rows", "cols"),
        ),
        out_specs=(P("rows", "cols"), P(None, "cols"), P("cols"), P("rows", "cols")),
        check_vma=False,
    )
```

time: 37.4 us -> 35.3 us (0.944)
  Pallas kernels: 36.1 us -> 34 us
    pallas_call x1, Pallas kernels: 35.4 us -> 33.3 us  [local(): pl.pallas_call(functools.partial(layer_kernel, plan), out_shape=tuple((pl...]
where the time goes in v3:
time: 35.3 us; the launch traced here: 35.2 us
  Pallas kernels  34 us (96%)
  between operations  1.29 us (4%)
    pallas_call x1, Pallas kernels, local(): pl.pallas_call(functools.partial(layer_kernel, plan), out_shape=tuple((pl...  33.3 us

profile of v3, /device:TPU:1, one launch (start us, length us, event | category | flops | bytes accessed | tf_op | source)
XLA Modules:
  0.0 35.2 jit_solution(3816835664184196293)
XLA Ops:
  1.3 33.3 %graph_layer.1 = (bf16[256,128]{1,0:T(8,128)(2,1)S(1)}, f32[128,128]{1,0:T(8,128)S(1)}, f32[1,128]{1,0:T(1,128)S(1)}, bf16[64,256]{1,0:T(8,128)(2,1)S(1)}) custom-call(s32[96]{0:T(128)} %src_hbm.1, s32[96]{0:T(128)} %dst_hbm.1, s32[1]{0:T(128)S(6)} %copy.13.count_ref, s32[2]{0:T(128)} %size_hbm.1, bf16[64,256]{1,0:T(8,128)(2,1)} %bitcast.4, ...), custom_call_target="tpu_custom_call" | custom-call | tf_op jit(solution)/shard_map/graph_layer/pallas_call | solution.py:457
  34.5 0.7 %write_results.1 = (bf16[256,128]{1,0:T(8,128)(2,1)}, f32[128,128]{1,0:T(8,128)}, f32[1,128]{1,0:T(1,128)}, bf16[64,256]{1,0:T(8,128)(2,1)}) custom-call(bf16[256,128]{1,0:T(8,128)(2,1)S(1)} %get-tuple-element.12.refs_0_, f32[128,128]{1,0:T(8,128)S(1)} %get-tuple-element.13.refs_1_, f32[1,128]{1,0:T(1,128)S(1)} %get-tuple-element.14.refs_2_, ...), custom_call_target="tpu_custom_call" | custom-call | tf_op jit(solution)/shard_map/write_results/pallas_call | solution.py:521

commit v4 on v3

--- a/solution.py
+++ b/solution.py
@@ -78,7 +78,6 @@
     fold_in,
     fold_mid,
     fold_all,
-    bias_in,
     bias_mid,
     give,
     take,
@@ -99,8 +98,6 @@
     r2_recv,
     r3_send,
     r3_recv,
-    b1_send,
-    b1_recv,
     b2_send,
     b2_recv,
 ):
@@ -117,7 +114,7 @@
     across = [k for k in range(levels + 1) if k not in relayed]
     far_near = sorted(range(levels), key=lambda k: -reach(near[k]))
     far_wide = sorted(range(1, wide_count), key=lambda m: -reach(wide[m]))
-    far_deep = sorted(range(1, deep_count), key=lambda m: -reach(deep[m]))
+    far_deep = sorted(range(1, deep_count), key=lambda m: (-(deep[m] & 8), -reach(deep[m])))
     parts = tile_sem.shape[0]
     part_slots = slots // parts
 
@@ -286,10 +283,10 @@
     wide_feat, units = gw_ref.shape
     chunk = wide_feat // wide_count
     for j in range(wide_count):
-        stage[j] = grad_weight[j * chunk : (j + 1) * chunk]
+        stage[j, :chunk] = grad_weight[j * chunk : (j + 1) * chunk]
+        stage[j, chunk:] = grad_weight[wide_feat : wide_feat + 8]
     my_wide, my_deep = me.place(wide), me.place(deep)
-    bias_in[my_wide] = grad_weight[wide_feat : wide_feat + 1]
-    scatter_copies, bias_copies = [], []
+    scatter_copies = []
     for m in far_wide:
         scatter_copies.append(
             remote(
@@ -300,17 +297,7 @@
                 wide[m],
             )
         )
-        bias_copies.append(
-            remote(
-                bias_in.at[my_wide],
-                bias_in.at[my_wide],
-                b1_send.at[m],
-                b1_recv.at[m],
-                wide[m],
-            )
-        )
         scatter_copies[-1].start()
-        bias_copies[-1].start()
     fold_in[my_wide] = stage[my_wide]
 
     part_back[...] = jnp.dot(weights[...], grad, preferred_element_type=F32)
@@ -325,14 +312,11 @@
         remote(
             stage.at[0], fold_in.at[there], r1_send.at[m], r1_recv.at[m], wide[m]
         ).wait_recv()
-        remote(
-            bias_in.at[there], bias_in.at[there], b1_send.at[m], b1_recv.at[m], wide[m]
-        ).wait_recv()
-    part, bias_part = fold_in[0], bias_in[0]
+    part = fold_in[0]
     for m in range(1, wide_count):
-        part, bias_part = part + fold_in[m], bias_part + bias_in[m]
-    fold_mid[my_deep] = part.astype(fold_mid.dtype)
-    bias_mid[my_deep] = bias_part
+        part = part + fold_in[m]
+    fold_mid[my_deep] = part[:chunk].astype(fold_mid.dtype)
+    bias_mid[my_deep] = part[chunk : chunk + 1]
     deep_copies = []
     for m in far_deep:
         for fold, send, recv in ((fold_mid, r2_send, r2_recv), (bias_mid, b2_send, b2_recv)):
@@ -392,7 +376,6 @@
         list(feature_copies.values())
         + relays
         + scatter_copies
-        + bias_copies
         + [half_copy]
         + back_copies
         + deep_copies
@@ -478,11 +461,10 @@
                 pltpu.VMEM((units, nodes), F32),
                 pltpu.VMEM((wide_feat, nodes), F32),
                 pltpu.VMEM((half, nodes), F32),
-                pltpu.VMEM((len(wide), chunk, units), F32),
-                pltpu.VMEM((len(wide), chunk, units), F32),
+                pltpu.VMEM((len(wide), chunk + 8, units), F32),
+                pltpu.VMEM((len(wide), chunk + 8, units), F32),
                 pltpu.VMEM((len(deep), chunk, units), MID),
                 pltpu.VMEM((len(wide), chunk, units), F32),
-                pltpu.VMEM((len(wide), 1, units), F32),
                 pltpu.VMEM((len(deep), 1, units), F32),
                 pltpu.VMEM((levels, half, nodes), BF16),
                 pltpu.VMEM((levels, half, nodes), BF16),
@@ -503,8 +485,6 @@
                 dma((len(deep),)),
                 dma((len(wide),)),
                 dma((len(wide),)),
-                dma((len(wide),)),
-                dma((len(wide),)),
                 dma((len(deep),)),
                 dma((len(deep),)),
             ],

time: 35.3 us -> 35.2 us (level)
  no operation moved by 1% of the time
where the time goes in v4:
time: 35.2 us; the launch traced here: 35.1 us
  Pallas kernels  33.9 us (96%)
  between operations  1.29 us (4%)
    pallas_call x1, Pallas kernels, local(): pl.pallas_call(functools.partial(layer_kernel, plan), out_shape=tuple((pl...  33.2 us

profile of v4, /device:TPU:1, one launch (start us, length us, event | category | flops | bytes accessed | tf_op | source)
XLA Modules:
  0.0 35.1 jit_solution(11203492301745010196)
XLA Ops:
  1.3 33.2 %graph_layer.1 = (bf16[256,128]{1,0:T(8,128)(2,1)S(1)}, f32[128,128]{1,0:T(8,128)S(1)}, f32[1,128]{1,0:T(1,128)S(1)}, bf16[64,256]{1,0:T(8,128)(2,1)S(1)}) custom-call(s32[96]{0:T(128)} %src_hbm.1, s32[96]{0:T(128)} %dst_hbm.1, s32[1]{0:T(128)S(6)} %copy.13.count_ref, s32[2]{0:T(128)} %size_hbm.1, bf16[64,256]{1,0:T(8,128)(2,1)} %bitcast.4, ...), custom_call_target="tpu_custom_call" | custom-call | tf_op jit(solution)/shard_map/graph_layer/pallas_call | solution.py:440
  34.4 0.7 %write_results.1 = (bf16[256,128]{1,0:T(8,128)(2,1)}, f32[128,128]{1,0:T(8,128)}, f32[1,128]{1,0:T(1,128)}, bf16[64,256]{1,0:T(8,128)(2,1)}) custom-call(bf16[256,128]{1,0:T(8,128)(2,1)S(1)} %get-tuple-element.12.refs_0_, f32[128,128]{1,0:T(8,128)S(1)} %get-tuple-element.13.refs_1_, f32[1,128]{1,0:T(1,128)S(1)} %get-tuple-element.14.refs_2_, ...), custom_call_target="tpu_custom_call" | custom-call | tf_op jit(solution)/shard_map/write_results/pallas_call | solution.py:501

commit v5 on v4

--- a/solution.py
+++ b/solution.py
@@ -13,7 +13,7 @@
 MESH = pl.DeviceIdType.MESH
 PARTS = 4
 MID = jnp.bfloat16
-RELAY = 0
+RELAY = (1, 16)
 
 
 class Spot:
@@ -110,7 +110,7 @@
     half, nodes = feat.shape
     own_rows = pl.ds(pl.multiple_of(col * half, half), half)
     other_rows = pl.ds(pl.multiple_of((1 - col) * half, half), half)
-    relayed = [k for k in range(levels) if reach(near[k]) <= RELAY]
+    relayed = [k for k in range(levels) if near[k] in RELAY]
     across = [k for k in range(levels + 1) if k not in relayed]
     far_near = sorted(range(levels), key=lambda k: -reach(near[k]))
     far_wide = sorted(range(1, wide_count), key=lambda m: -reach(wide[m]))

time: 35.2 us -> 35.2 us (level)
  no operation moved by 1% of the time
where the time goes in v5:
time: 35.2 us; the launch traced here: 35.1 us
  Pallas kernels  33.9 us (96%)
  between operations  1.29 us (4%)
    pallas_call x1, Pallas kernels, local(): pl.pallas_call(functools.partial(layer_kernel, plan), out_shape=tuple((pl...  33.2 us

profile of v5, /device:TPU:1, one launch (start us, length us, event | category | flops | bytes accessed | tf_op | source)
XLA Modules:
  0.0 35.1 jit_solution(4433094008337913226)
XLA Ops:
  1.3 33.2 %graph_layer.1 = (bf16[256,128]{1,0:T(8,128)(2,1)S(1)}, f32[128,128]{1,0:T(8,128)S(1)}, f32[1,128]{1,0:T(1,128)S(1)}, bf16[64,256]{1,0:T(8,128)(2,1)S(1)}) custom-call(s32[96]{0:T(128)} %src_hbm.1, s32[96]{0:T(128)} %dst_hbm.1, s32[1]{0:T(128)S(6)} %copy.13.count_ref, s32[2]{0:T(128)} %size_hbm.1, bf16[64,256]{1,0:T(8,128)(2,1)} %bitcast.4, ...), custom_call_target="tpu_custom_call" | custom-call | tf_op jit(solution)/shard_map/graph_layer/pallas_call | solution.py:440
  34.4 0.7 %write_results.1 = (bf16[256,128]{1,0:T(8,128)(2,1)}, f32[128,128]{1,0:T(8,128)}, f32[1,128]{1,0:T(1,128)}, bf16[64,256]{1,0:T(8,128)(2,1)}) custom-call(bf16[256,128]{1,0:T(8,128)(2,1)S(1)} %get-tuple-element.12.refs_0_, f32[128,128]{1,0:T(8,128)S(1)} %get-tuple-element.13.refs_1_, f32[1,128]{1,0:T(1,128)S(1)} %get-tuple-element.14.refs_2_, ...), custom_call_target="tpu_custom_call" | custom-call | tf_op jit(solution)/shard_map/write_results/pallas_call | solution.py:501

commit v6 on v4

--- a/solution.py
+++ b/solution.py
@@ -318,8 +318,14 @@
     fold_mid[my_deep] = part[:chunk].astype(fold_mid.dtype)
     bias_mid[my_deep] = part[chunk : chunk + 1]
     deep_copies = []
-    for m in far_deep:
-        for fold, send, recv in ((fold_mid, r2_send, r2_recv), (bias_mid, b2_send, b2_recv)):
+    first = len(far_deep) // 4
+    for fold, send, recv, which in (
+        (fold_mid, r2_send, r2_recv, far_deep[:first]),
+        (bias_mid, b2_send, b2_recv, far_deep[:first]),
+        (fold_mid, r2_send, r2_recv, far_deep[first:]),
+        (bias_mid, b2_send, b2_recv, far_deep[first:]),
+    ):
+        for m in which:
             deep_copies.append(
                 remote(fold.at[my_deep], fold.at[my_deep], send.at[m], recv.at[m], deep[m])
             )

time: 35.2 us -> 35.2 us (level)
  no operation moved by 1% of the time
where the time goes in v6:
time: 35.2 us; the launch traced here: 35.1 us
  Pallas kernels  33.8 us (96%)
  between operations  1.29 us (4%)
    pallas_call x1, Pallas kernels, local(): pl.pallas_call(functools.partial(layer_kernel, plan), out_shape=tuple((pl...  33.1 us

profile of v6, /device:TPU:1, one launch (start us, length us, event | category | flops | bytes accessed | tf_op | source)
XLA Modules:
  0.0 35.1 jit_solution(1045768459877435224)
XLA Ops:
  1.3 33.1 %graph_layer.1 = (bf16[256,128]{1,0:T(8,128)(2,1)S(1)}, f32[128,128]{1,0:T(8,128)S(1)}, f32[1,128]{1,0:T(1,128)S(1)}, bf16[64,256]{1,0:T(8,128)(2,1)S(1)}) custom-call(s32[96]{0:T(128)} %src_hbm.1, s32[96]{0:T(128)} %dst_hbm.1, s32[1]{0:T(128)S(6)} %copy.13.count_ref, s32[2]{0:T(128)} %size_hbm.1, bf16[64,256]{1,0:T(8,128)(2,1)} %bitcast.4, ...), custom_call_target="tpu_custom_call" | custom-call | tf_op jit(solution)/shard_map/graph_layer/pallas_call | solution.py:446
  34.4 0.7 %write_results.1 = (bf16[256,128]{1,0:T(8,128)(2,1)}, f32[128,128]{1,0:T(8,128)}, f32[1,128]{1,0:T(1,128)}, bf16[64,256]{1,0:T(8,128)(2,1)}) custom-call(bf16[256,128]{1,0:T(8,128)(2,1)S(1)} %get-tuple-element.12.refs_0_, f32[128,128]{1,0:T(8,128)S(1)} %get-tuple-element.13.refs_1_, f32[1,128]{1,0:T(1,128)S(1)} %get-tuple-element.14.refs_2_, ...), custom_call_target="tpu_custom_call" | custom-call | tf_op jit(solution)/shard_map/write_results/pallas_call | solution.py:507
